TPU v7x, 512 devices: a whole 4x4x16 slice. The times are simulated.
512 devices in a mesh: dp: 64 (over x_lo, z, core), tensor: 8 (over y, x_hi).
Axes of the slice: x: 4 (x_hi: 2, x_lo: 2; x = x_hi * 2 + x_lo), y: 4, z: 16, core: 2. Of those that a mesh axis runs over, the one named last changes fastest.
Arguments:
- hidden_acts: bfloat16 [512, 128, 14336], P('dp', None, 'tensor'), may hold values from -6 to 6
- out_grads: bfloat16 [512, 128, 4096], P('dp', None, 'tensor'), may hold values from -1.25 to 1.25
- proj_in: bfloat16 [14336, 64], P('tensor'), may hold values from -0.046875 to 0.046875
- proj_out: bfloat16 [4096, 64], P('tensor'), may hold values from -0.09375 to 0.09375
- queries: bfloat16 [1024, 4096], P('dp'), may hold values from -6 to 6
Outputs:
- train_grads: bfloat16 [512, 4096], P(('dp', 'tensor'))
- scores: float32 [512, 1024], P(('dp', 'tensor'))
All inputs are finite; a program needn't handle non-finite values.
Results may differ from a plain program's by a relative error of at most 0.0057.
Values may be sent and summed in bfloat16 or wider, within the bound.
A program may use at most 64 MiB of HBM per device.

v0:
```python
import jax
import jax.numpy as jnp
from jax import lax
from jax.sharding import PartitionSpec as P


def local(hidden_acts, out_grads, proj_in, proj_out, queries):
    rank_size = proj_in.shape[1]
    side_in = jnp.einsum("esf,fr->esr", hidden_acts, proj_in, preferred_element_type=jnp.float32)
    side_out = jnp.einsum("esf,fr->esr", out_grads, proj_out, preferred_element_type=jnp.float32)
    summed = lax.psum_scatter(
        jnp.concatenate([side_out, side_in], axis=2), "tensor", scatter_dimension=0, tiled=True
    )
    grad_proj = summed[:, :, :rank_size].astype(jnp.bfloat16)
    act_proj = summed[:, :, rank_size:].astype(jnp.bfloat16)
    outer = jnp.einsum("esi,esj->eij", grad_proj, act_proj, preferred_element_type=jnp.float32)
    train_grads = outer.reshape(outer.shape[0], rank_size * rank_size).astype(jnp.bfloat16)
    scores = (
        jnp.einsum(
            "ek,qk->eq",
            train_grads,
            lax.all_gather(queries, "dp", axis=0, tiled=True),
            preferred_element_type=jnp.float32,
        )
        / rank_size
    )
    return (train_grads, scores)


def solution(mesh):
    in_specs = (
        P("dp", None, "tensor"),
        P("dp", None, "tensor"),
        P("tensor", None),
        P("tensor", None),
        P("dp", None),
    )
    out_specs = (P(("dp", "tensor"), None), P(("dp", "tensor"), None))
    return jax.shard_map(local, mesh=mesh, in_specs=in_specs, out_specs=out_specs, check_vma=False)
```

profile of v0, /device:TPU:1, one launch (start us, length us, event | category | flops | bytes accessed | tf_op | source)
XLA Modules:
  0.0 165.8 jit_solution(16795613261362063778)
XLA Ops:
  8.0 0.0 copy-start
  8.0 0.0 reduce-scatter.2.cloned.1.call-start
  8.1 3.3 %fusion = f32[8,128,64]{1,2,0:T(8,128)S(1)} fusion(bf16[8,128,1792]{2,1,0:T(8,128)(2,1)} %param.5, bf16[1792,64]{0,1:T(8,128)(2,1)} %param.7), kind=kOutput, calls=%fused_computation.2 | convolution fusion | flops 234881024 | bytes 4161536 | tf_op jit(solution)/shard_map/esf,fr->esr/dot_general | solution.py:9
  11.4 0.0 copy-done
  11.4 1.3 fusion.2
  12.7 0.9 pad_maximum_fusion
  13.6 0.0 reduce-scatter.2.cloned.1.call-update
  13.6 0.0 all-gather.2.cloned.1.call-start
  13.6 0.5 all-gather.2.cloned.1.call-update
  14.2 88.8 %reduce-scatter.2.cloned.1.call-done = f32[1,128,128]{1,2,0:T(8,128)} async-done(((f32[8,128,128]{1,2,0:T(8,128)}), f32[1,128,128]{1,2,0:T(8,128)}) %reduce-scatter.2.cloned.1.call-update) | async-done | bytes 65552 | tf_op jit(solution)/shard_map/reduce_scatter | solution.py:11
  103.0 0.8 convert.4
  103.9 0.1 convolution_convert_fusion
  104.0 0.1 reshape.35
  104.1 0.7 convert_element_type.21
  104.8 47.3 %all-gather.2.cloned.1.call-done = bf16[1024,4096]{1,0:T(8,128)(2,1)} async-done(((bf16[16,4096]{1,0:T(8,128)(2,1)}), bf16[1024,4096]{1,0:T(8,128)(2,1)}) %all-gather.2.cloned.1.call-update) | async-done | bytes 8388624 | tf_op jit(solution)/shard_map/all_gather | solution.py:22
  152.1 5.6 %fusion.4 = f32[1,1024]{1,0:T(1,128)S(1)} fusion(bf16[4096,1]{0,1:T(2,128)(2,1)S(1)} %reshape.35, bf16[1024,4096]{1,0:T(8,128)(2,1)} %all-gather.2.cloned.1.call-done), kind=kOutput, calls=%fused_computation.9 | convolution fusion | flops 8388608 | bytes 8400896 | tf_op jit(solution)/shard_map/ek,qk->eq/dot_general | solution.py:19
  157.7 0.6 broadcast_multiply_fusion
Async XLA Ops:
  8.0 3.4 %copy-start = (bf16[8,128,512]{2,1,0:T(8,128)(2,1)S(1)}, bf16[8,128,512]{2,1,0:T(8,128)(2,1)}, u32[]{:S(2)}) copy-start(bf16[8,128,512]{2,1,0:T(8,128)(2,1)} %param.6) | copy-start | bytes 3145732
  8.0 95.0 %reduce-scatter.2.cloned.1.call-start = ((), (), s32[]{:S(2)}) async-start(), calls=%async_computation.1 | async-start | bytes 589824 | tf_op jit(solution)/shard_map/reduce_scatter | solution.py:11
  13.6 138.5 %all-gather.2.cloned.1.call-start = ((), (), s32[]{:S(2)}) async-start(), calls=%async_computation.2 | async-start | bytes 8519680 | tf_op jit(solution)/shard_map/all_gather | solution.py:22
Sparse Core Ops, SparseCore 0:
  13.7 89.2 reduce-scatter.1
Sparse Core Ops, SparseCore 1:
  16.4 135.6 all-gather.1
where the time goes:
time: 166 us
  waiting for transfers between devices  137 us (83%)
  between operations  15.5 us (9%)
  matrix products  10.4 us (6%)
  other arithmetic  2.35 us (1%)
    reduce_scatter x1, waiting for transfers between devices, local(): lax.psum_scatter(jnp.concatenate([side_out, side_in], axis=2), 'tensor',...  88.8 us
    all_gather x1, waiting for transfers between devices, local(): lax.all_gather(queries, 'dp', axis=0, tiled=True)  47.3 us
    dot_general x1, matrix products, local(): jnp.einsum('ek,qk->eq', train_grads, lax.all_gather(queries, 'dp', axis=0...  5.64 us
    dot_general x1, matrix products, local(): jnp.einsum('esf,fr->esr', hidden_acts, proj_in, preferred_element_type=jn...  3.33 us
  transfers between devices with their start and end apart: 2, of which 2 were waited for; matrix products, arithmetic and copies ran while one was open for 1% of the time, Pallas kernels for 0%

commit v1 on v0

v1 whole, which is shorter than its diff:
```python
import functools

import jax
import jax.numpy as jnp
from jax import lax
from jax.experimental import pallas as pl
from jax.experimental.pallas import tpu as pltpu
from jax.sharding import PartitionSpec as P

MESH = pl.DeviceIdType.MESH
SIZES = dict(x_lo=2, z=16, core=2, y=4, x_hi=2)
F32, BF16 = jnp.float32, jnp.bfloat16

TENSOR = [(2, 1), (1, 1), (3, 1), (2, 0), (0, 1), (1, 0), (3, 0), (0, 0)]
PLANE = [(y, h, l, c) for y, h in TENSOR for l in (1, 0) for c in (1, 0)]
OPPOSITE = (2, 1, 0, 0)


def position():
    dp, tensor = lax.axis_index("dp"), lax.axis_index("tensor")
    return dict(
        x_lo=dp // 32, z=lax.rem(dp // 2, 16), core=lax.rem(dp, 2), y=tensor // 2, x_hi=lax.rem(tensor, 2)
    )


def at(place, **offsets):
    moved = {k: lax.rem(v + offsets.get(k, 0) + SIZES[k], SIZES[k]) for k, v in place.items()}
    return {
        "dp": moved["x_lo"] * 32 + moved["z"] * 2 + moved["core"],
        "tensor": moved["y"] * 2 + moved["x_hi"],
    }


def in_plane(place, offset):
    return at(place, **dict(zip(("y", "x_hi", "x_lo", "core"), offset)))


def nt(a, b):
    return lax.dot_general(a, b, (((1,), (1,)), ((), ())), preferred_element_type=F32)


def kernel(
    hidden, grads, w_in, w_out, queries, tg_out, scores_out,
    h_buf, g_buf, win_buf, wout_raw, wout_f32, wout_buf,
    part_send, part_recv, own_part,
    t_send, t_recv, tg_send, tg_recv, q_buf, s_send, s_recv,
    h_sem, g_sem, w_sem,
    part_ssem, part_rsem, t_ssem, t_rsem, tg_ssem, tg_rsem,
    q_ssem, q_rsem, far_ssem, far_rsem, sib_ssem, fwd_ssem, s_ssem, s_rsem,
):
    me = position()
    tensor = lax.axis_index("tensor")

    loads = [
        pltpu.make_async_copy(w_out, wout_raw, w_sem.at[0]),
        pltpu.make_async_copy(w_in, win_buf, w_sem.at[1]),
    ]
    for c in loads:
        c.start()
    reads = []
    for k, (y, h) in enumerate(TENSOR):
        example = lax.rem(me["y"] + y + 2, 4) * 2 + lax.rem(me["x_hi"] + h + 1, 2)
        pair = (
            pltpu.make_async_copy(grads.at[example], g_buf.at[k], g_sem.at[k]),
            pltpu.make_async_copy(hidden.at[example], h_buf.at[k], h_sem.at[k]),
        )
        for c in pair:
            c.start()
        reads.append(pair)

    barrier = pltpu.get_barrier_semaphore()
    for off in PLANE[:-1]:
        pl.semaphore_signal(barrier, inc=1, device_id=in_plane(me, off), device_id_type=MESH)
    for d in (4, -4, 3, -3, 2, -2, 1, -1):
        for c in (0, 1):
            pl.semaphore_signal(barrier, inc=1, device_id=at(me, z=d, core=c), device_id_type=MESH)

    loads[0].wait()
    for j in range(4):
        lanes = slice(128 * j, 128 * j + 128)
        wout_f32[j] = wout_raw[:, lanes].astype(F32)
        wout_buf[0:32, lanes] = wout_f32[j, pl.ds(0, 32, stride=2), :].astype(BF16)
        wout_buf[32:64, lanes] = wout_f32[j, pl.ds(1, 32, stride=2), :].astype(BF16)
    loads[1].wait()

    def partial(k):
        for c in reads[k]:
            c.wait()
        return nt(wout_buf[...], g_buf[k]), nt(win_buf[...], h_buf[k])

    for k in range(7):
        a, b = partial(k)
        part_send[k, 0:64, :] = a.astype(BF16)
        part_send[k, 64:128, :] = b.astype(BF16)
        if k == EARLY - 1:
            pl.semaphore_wait(barrier, 47)
            for j in range(k):
                send_part(j, me, part_send, part_recv, part_ssem, part_rsem).start()
        if k >= EARLY - 1:
            send_part(k, me, part_send, part_recv, part_ssem, part_rsem).start()
        if k == EARLY - 1:
            half = me["z"] // 8
            slot = lax.rem(me["z"], 8) * 2 + me["core"]
            mine = queries.at[:, pl.ds(pl.multiple_of(tensor * 512, 512), 512)]

            def near(d, ssem, rsem):
                target = at(dict(me, core=half), z=d)
                return pltpu.make_async_remote_copy(
                    mine, q_buf.at[slot], ssem, rsem, device_id=target, device_id_type=MESH
                )

            for d in (4, -4):
                near(d, far_ssem, far_rsem).start()
            for d in (3, -3, 2, -2, 1, -1):
                near(d, q_ssem, q_rsem).start()
            sibling = near(0, sib_ssem, q_rsem)
            own = pltpu.make_async_copy(mine, q_buf.at[slot], q_rsem)

            @pl.when(half == me["core"])
            def _():
                own.start()

            @pl.when(half != me["core"])
            def _():
                sibling.start()

    a, b = partial(7)
    own_part[0:64, :] = a
    own_part[64:128, :] = b

    back = lax.rem(me["z"] + 12, 16)
    up = (back // 8) == me["core"]
    sign = jnp.where(up, 1, -1)
    source = lax.rem(me["z"] - 4 * sign + 16, 16)
    first = lax.rem(source, 8) * 2
    pltpu.make_async_copy(q_buf.at[pl.ds(0, 2)], q_buf.at[pl.ds(0, 2)], far_rsem).wait()
    for c, d in ((0, 3), (1, 3), (0, 2), (1, 2), (0, 1), (1, 1), (None, 4)):
        block = first + (jnp.where(up, 0, 1) if c is None else c)
        pltpu.make_async_remote_copy(
            q_buf.at[block], q_buf.at[block], fwd_ssem, q_rsem,
            device_id=at(me, z=sign * d), device_id_type=MESH,
        ).start()

    pltpu.make_async_copy(part_recv, part_recv, part_rsem).wait()
    total = own_part[...]
    for k in range(7):
        total += part_recv[k].astype(F32)
    total = total.astype(BF16)
    act = total[64:128]
    both = nt(total[0:64], jnp.concatenate([act, act], axis=0))
    lane = lax.broadcasted_iota(jnp.int32, (32, 128), 1)
    rows = jnp.where(lane < 64, both[0:32], both[32:64]).astype(BF16)
    tg_send[...] = rows
    wide = rows.astype(F32)
    for k in range(8):
        t_send[k] = wide[4 * k : 4 * k + 4]

    for s, off in enumerate(PLANE[:-1]):
        target = in_plane(me, off)
        pltpu.make_async_remote_copy(
            t_send.at[target["tensor"]], t_recv.at[s], t_ssem, t_rsem, device_id=target, device_id_type=MESH
        ).start()
    pltpu.make_async_copy(t_send.at[tensor], t_recv.at[31], t_rsem).start()
    whole = pltpu.make_async_remote_copy(
        tg_send, tg_recv, tg_ssem, tg_rsem, device_id=in_plane(me, OPPOSITE), device_id_type=MESH
    )
    whole.start()

    pltpu.make_async_copy(q_buf.at[pl.ds(0, 14)], q_buf.at[pl.ds(0, 14)], q_rsem).wait()
    pltpu.make_async_copy(t_recv, t_recv, t_rsem).wait()
    x = jnp.concatenate([t_recv[:, k, :] for k in range(4)], axis=1).astype(BF16)
    part = nt(x, q_buf[...].reshape(256, 512)) * (1.0 / 64)
    for k in range(2):
        s_send[:, k, :] = part[:, 128 * k : 128 * k + 128]
    place = (me["x_lo"] * 2 + me["core"]) * 8 + tensor
    for s, off in enumerate(PLANE):
        if off == OPPOSITE:
            pltpu.make_async_copy(s_send.at[s], s_recv.at[place], s_rsem).start()
            continue
        back = tuple(o - p for o, p in zip(OPPOSITE, off))
        pltpu.make_async_remote_copy(
            s_send.at[s], s_recv.at[place], s_ssem, s_rsem, device_id=in_plane(me, back), device_id_type=MESH
        ).start()

    pltpu.make_async_copy(part_send, part_send, part_ssem).wait()
    pltpu.make_async_copy(t_recv.at[pl.ds(0, 31)], t_recv.at[pl.ds(0, 31)], t_ssem).wait()
    whole.wait_send()
    pltpu.make_async_copy(q_buf.at[pl.ds(0, 2)], q_buf.at[pl.ds(0, 2)], far_ssem).wait()
    pltpu.make_async_copy(q_buf.at[pl.ds(0, 6)], q_buf.at[pl.ds(0, 6)], q_ssem).wait()
    pltpu.make_async_copy(q_buf.at[pl.ds(0, 7)], q_buf.at[pl.ds(0, 7)], fwd_ssem).wait()

    @pl.when(half != me["core"])
    def _():
        sibling.wait_send()

    whole.wait_recv()
    tg_out[...] = tg_recv[...]

    pltpu.make_async_copy(s_recv, s_recv, s_rsem).wait()
    for w in range(4):
        scores_out[2 * w : 2 * w + 2, :] = jnp.sum(s_recv[8 * w : 8 * w + 8], axis=0)
    pltpu.make_async_copy(s_recv.at[pl.ds(0, 31)], s_recv.at[pl.ds(0, 31)], s_ssem).wait()


EARLY = 3


def send_part(k, me, part_send, part_recv, ssem, rsem):
    y, h = TENSOR[k]
    return pltpu.make_async_remote_copy(
        part_send.at[k], part_recv.at[k], ssem, rsem, device_id=at(me, y=y, x_hi=h), device_id_type=MESH
    )


def local(hidden_acts, out_grads, proj_in, proj_out, queries):
    dma = pltpu.SemaphoreType.DMA
    tg, scores = pl.pallas_call(
        kernel,
        name="influence",
        out_shape=(jax.ShapeDtypeStruct((32, 128), BF16), jax.ShapeDtypeStruct((8, 128), F32)),
        in_specs=[pl.BlockSpec(memory_space=pl.ANY)] * 5,
        out_specs=(pl.BlockSpec(memory_space=pltpu.VMEM),) * 2,
        scratch_shapes=[
            pltpu.VMEM((8, 128, 1792), BF16),
            pltpu.VMEM((8, 128, 512), BF16),
            pltpu.VMEM((64, 1792), BF16),
            pltpu.VMEM((64, 512), BF16),
            pltpu.VMEM((4, 64, 128), F32),
            pltpu.VMEM((64, 512), BF16),
            pltpu.VMEM((7, 128, 128), BF16),
            pltpu.VMEM((7, 128, 128), BF16),
            pltpu.VMEM((128, 128), F32),
            pltpu.VMEM((8, 4, 128), F32),
            pltpu.VMEM((32, 4, 128), F32),
            pltpu.VMEM((32, 128), BF16),
            pltpu.VMEM((32, 128), BF16),
            pltpu.VMEM((16, 16, 512), BF16),
            pltpu.VMEM((32, 2, 128), F32),
            pltpu.VMEM((32, 2, 128), F32),
            dma((8,)), dma((8,)), dma((2,)),
        ] + [dma] * 14,
        compiler_params=pltpu.CompilerParams(
            collective_id=0, has_side_effects=True, vmem_limit_bytes=56 * 1024 * 1024
        ),
    )(hidden_acts, out_grads, proj_in.T, proj_out.T, queries)
    return tg.reshape(1, 4096), scores.reshape(1, 1024)


def solution(mesh):
    in_specs = (
        P("dp", None, "tensor"),
        P("dp", None, "tensor"),
        P("tensor", None),
        P("tensor", None),
        P("dp", None),
    )
    out_specs = (P(("dp", "tensor"), None), P(("dp", "tensor"), None))
    return jax.shard_map(local, mesh=mesh, in_specs=in_specs, out_specs=out_specs, check_vma=False)
```

time: 166 us -> 36.6 us (0.22)
  waiting for transfers between devices: 137 us -> 0 us
  Pallas kernels: 0 us -> 33.1 us
  between operations: 15.5 us -> 0.64 us
  matrix products: 10.4 us -> 0 us
  other arithmetic: 2.35 us -> 0 us
  local copies, waits for them, and re-layouts: 0.81 us -> 2.58 us
    reduce_scatter x1 -> x0, waiting for transfers between devices: 88.8 us -> none  [local(): lax.psum_scatter(jnp.concatenate([side_out, side_in], axis=2), 'tensor',...]
    all_gather x1 -> x0, waiting for transfers between devices: 47.3 us -> none  [local(): lax.all_gather(queries, 'dp', axis=0, tiled=True)]
    pallas_call x0 -> x1, Pallas kernels: none -> 33.1 us  [local(): pl.pallas_call(kernel, name='influence', out_shape=(jax.ShapeDtypeStruct(...]
    dot_general x4 -> x0, matrix products: 10.4 us -> none  [the longest x1 5.64 us: local(): jnp.einsum('ek,qk->eq', train_grads, lax.all_gather(queries, 'dp', axis=0...]
    unnamed x2, local copies, waits for them, and re-layouts: 0.01 us -> 2.58 us
  transfers between devices with their start and end apart: 2 -> 0, of which waited for: 2 -> 0; matrix products, arithmetic and copies ran while one was open for 1% -> 0% of each run, Pallas kernels for 0% -> 0%
where the time goes in v1:
time: 36.6 us; the launch traced here: 36.4 us
  Pallas kernels  33.1 us (90%)
  local copies, waits for them, and re-layouts  2.58 us (7%)
  between operations  0.64 us (2%)
    pallas_call x1, Pallas kernels, local(): pl.pallas_call(kernel, name='influence', out_shape=(jax.ShapeDtypeStruct(...  33.1 us
    unnamed x2, local copies, waits for them, and re-layouts  2.58 us

profile of v1, /device:TPU:1, one launch (start us, length us, event | category | flops | bytes accessed | tf_op | source)
XLA Modules:
  0.0 36.4 jit_solution(6080013423354095930)
XLA Ops:
  0.6 33.1 %influence.1 = (bf16[32,128]{1,0:T(8,128)(2,1)}, f32[8,128]{1,0:T(8,128)}) custom-call(bf16[8,128,1792]{2,1,0:T(8,128)(2,1)} %hidden.1, bf16[8,128,512]{2,1,0:T(8,128)(2,1)} %grads.1, bf16[64,1792]{1,0:T(8,128)(2,1)} %bitcast.8, bf16[64,512]{1,0:T(8,128)(2,1)} %bitcast.9, bf16[16,4096]{1,0:T(8,128)(2,1)} %queries.1), custom_call_target="tpu_custom_call" | custom-call | tf_op jit(solution)/shard_map/influence/pallas_call | solution.py:217
  33.8 1.3 %copy.9 = bf16[1,1,32,128]{3,1,2,0:T(2,128)(2,1)} copy(bf16[1,1,32,128]{3,2,1,0:T(8,128)(2,1)} %bitcast.11) | data formatting | bytes 16384
  35.1 1.3 %copy.11 = f32[1,1024]{1,0:T(1,128)} copy(f32[1,1024]{1,0:T(1,128)} %bitcast.12) | data formatting | bytes 8192

commit v2 on v1

--- a/solution.py
+++ b/solution.py
@@ -42,7 +42,7 @@
 def kernel(
     hidden, grads, w_in, w_out, queries, tg_out, scores_out,
     h_buf, g_buf, win_buf, wout_raw, wout_f32, wout_buf,
-    part_send, part_recv, own_part,
+    part_send, part_recv,
     t_send, t_recv, tg_send, tg_recv, q_buf, s_send, s_recv,
     h_sem, g_sem, w_sem,
     part_ssem, part_rsem, t_ssem, t_rsem, tg_ssem, tg_rsem,
@@ -58,11 +58,11 @@
     for c in loads:
         c.start()
     reads = []
-    for k, (y, h) in enumerate(TENSOR):
-        example = lax.rem(me["y"] + y + 2, 4) * 2 + lax.rem(me["x_hi"] + h + 1, 2)
+    for k in range(2):
+        four = pl.ds(4 * k, 4)
         pair = (
-            pltpu.make_async_copy(grads.at[example], g_buf.at[k], g_sem.at[k]),
-            pltpu.make_async_copy(hidden.at[example], h_buf.at[k], h_sem.at[k]),
+            pltpu.make_async_copy(grads.at[four], g_buf.at[four], g_sem.at[k]),
+            pltpu.make_async_copy(hidden.at[four], h_buf.at[four], h_sem.at[k]),
         )
         for c in pair:
             c.start()
@@ -83,50 +83,51 @@
         wout_buf[32:64, lanes] = wout_f32[j, pl.ds(1, 32, stride=2), :].astype(BF16)
     loads[1].wait()
 
-    def partial(k):
+    for k in range(2):
         for c in reads[k]:
             c.wait()
-        return nt(wout_buf[...], g_buf[k]), nt(win_buf[...], h_buf[k])
-
-    for k in range(7):
-        a, b = partial(k)
-        part_send[k, 0:64, :] = a.astype(BF16)
-        part_send[k, 64:128, :] = b.astype(BF16)
-        if k == EARLY - 1:
-            pl.semaphore_wait(barrier, 47)
-            for j in range(k):
-                send_part(j, me, part_send, part_recv, part_ssem, part_rsem).start()
-        if k >= EARLY - 1:
-            send_part(k, me, part_send, part_recv, part_ssem, part_rsem).start()
-        if k == EARLY - 1:
-            half = me["z"] // 8
-            slot = lax.rem(me["z"], 8) * 2 + me["core"]
-            mine = queries.at[:, pl.ds(pl.multiple_of(tensor * 512, 512), 512)]
-
-            def near(d, ssem, rsem):
-                target = at(dict(me, core=half), z=d)
-                return pltpu.make_async_remote_copy(
-                    mine, q_buf.at[slot], ssem, rsem, device_id=target, device_id_type=MESH
-                )
-
-            for d in (4, -4):
-                near(d, far_ssem, far_rsem).start()
-            for d in (3, -3, 2, -2, 1, -1):
-                near(d, q_ssem, q_rsem).start()
-            sibling = near(0, sib_ssem, q_rsem)
-            own = pltpu.make_async_copy(mine, q_buf.at[slot], q_rsem)
-
-            @pl.when(half == me["core"])
-            def _():
-                own.start()
-
-            @pl.when(half != me["core"])
-            def _():
-                sibling.start()
-
-    a, b = partial(7)
-    own_part[0:64, :] = a
-    own_part[64:128, :] = b
+        four = pl.ds(4 * k, 4)
+        a = nt(wout_buf[...], g_buf[four].reshape(512, 512)).astype(BF16)
+        b = nt(win_buf[...], h_buf[four].reshape(512, 1792)).astype(BF16)
+        for j in range(4):
+            part_send[4 * k + j, 0:64, :] = a[:, 128 * j : 128 * j + 128]
+            part_send[4 * k + j, 64:128, :] = b[:, 128 * j : 128 * j + 128]
+
+    pl.semaphore_wait(barrier, 47)
+    for k, (y, h) in enumerate(TENSOR):
+        example = lax.rem(me["y"] + y + 2, 4) * 2 + lax.rem(me["x_hi"] + h + 1, 2)
+        if k == 7:
+            pltpu.make_async_copy(part_send.at[example], part_recv.at[k], part_rsem).start()
+            continue
+        pltpu.make_async_remote_copy(
+            part_send.at[example], part_recv.at[k], part_ssem, part_rsem,
+            device_id=at(me, y=y, x_hi=h), device_id_type=MESH,
+        ).start()
+
+    half = me["z"] // 8
+    slot = lax.rem(me["z"], 8) * 2 + me["core"]
+    mine = queries.at[:, pl.ds(pl.multiple_of(tensor * 512, 512), 512)]
+
+    def near(d, ssem, rsem):
+        target = at(dict(me, core=half), z=d)
+        return pltpu.make_async_remote_copy(
+            mine, q_buf.at[slot], ssem, rsem, device_id=target, device_id_type=MESH
+        )
+
+    for d in (4, -4):
+        near(d, far_ssem, far_rsem).start()
+    for d in (3, -3, 2, -2, 1, -1):
+        near(d, q_ssem, q_rsem).start()
+    sibling = near(0, sib_ssem, q_rsem)
+    own = pltpu.make_async_copy(mine, q_buf.at[slot], q_rsem)
+
+    @pl.when(half == me["core"])
+    def _():
+        own.start()
+
+    @pl.when(half != me["core"])
+    def _():
+        sibling.start()
 
     back = lax.rem(me["z"] + 12, 16)
     up = (back // 8) == me["core"]
@@ -142,8 +143,8 @@
         ).start()
 
     pltpu.make_async_copy(part_recv, part_recv, part_rsem).wait()
-    total = own_part[...]
-    for k in range(7):
+    total = part_recv[0].astype(F32)
+    for k in range(1, 8):
         total += part_recv[k].astype(F32)
     total = total.astype(BF16)
     act = total[64:128]
@@ -182,7 +183,7 @@
             s_send.at[s], s_recv.at[place], s_ssem, s_rsem, device_id=in_plane(me, back), device_id_type=MESH
         ).start()
 
-    pltpu.make_async_copy(part_send, part_send, part_ssem).wait()
+    pltpu.make_async_copy(part_send.at[pl.ds(0, 7)], part_send.at[pl.ds(0, 7)], part_ssem).wait()
     pltpu.make_async_copy(t_recv.at[pl.ds(0, 31)], t_recv.at[pl.ds(0, 31)], t_ssem).wait()
     whole.wait_send()
     pltpu.make_async_copy(q_buf.at[pl.ds(0, 2)], q_buf.at[pl.ds(0, 2)], far_ssem).wait()
@@ -202,14 +203,9 @@
     pltpu.make_async_copy(s_recv.at[pl.ds(0, 31)], s_recv.at[pl.ds(0, 31)], s_ssem).wait()
 
 
-EARLY = 3
-
-
-def send_part(k, me, part_send, part_recv, ssem, rsem):
-    y, h = TENSOR[k]
-    return pltpu.make_async_remote_copy(
-        part_send.at[k], part_recv.at[k], ssem, rsem, device_id=at(me, y=y, x_hi=h), device_id_type=MESH
-    )
+def finish(tg, part, tg_out, scores_out):
+    tg_out[...] = tg[...].reshape(1, 4096)
+    scores_out[...] = part[...].reshape(1, 1024)
 
 
 def local(hidden_acts, out_grads, proj_in, proj_out, queries):
@@ -227,9 +223,8 @@
             pltpu.VMEM((64, 512), BF16),
             pltpu.VMEM((4, 64, 128), F32),
             pltpu.VMEM((64, 512), BF16),
-            pltpu.VMEM((7, 128, 128), BF16),
-            pltpu.VMEM((7, 128, 128), BF16),
-            pltpu.VMEM((128, 128), F32),
+            pltpu.VMEM((8, 128, 128), BF16),
+            pltpu.VMEM((8, 128, 128), BF16),
             pltpu.VMEM((8, 4, 128), F32),
             pltpu.VMEM((32, 4, 128), F32),
             pltpu.VMEM((32, 128), BF16),
@@ -237,13 +232,17 @@
             pltpu.VMEM((16, 16, 512), BF16),
             pltpu.VMEM((32, 2, 128), F32),
             pltpu.VMEM((32, 2, 128), F32),
-            dma((8,)), dma((8,)), dma((2,)),
+            dma((2,)), dma((2,)), dma((2,)),
         ] + [dma] * 14,
         compiler_params=pltpu.CompilerParams(
             collective_id=0, has_side_effects=True, vmem_limit_bytes=56 * 1024 * 1024
         ),
     )(hidden_acts, out_grads, proj_in.T, proj_out.T, queries)
-    return tg.reshape(1, 4096), scores.reshape(1, 1024)
+    return pl.pallas_call(
+        finish,
+        name="finish",
+        out_shape=(jax.ShapeDtypeStruct((1, 4096), BF16), jax.ShapeDtypeStruct((1, 1024), F32)),
+    )(tg, scores)
 
 
 def solution(mesh):

time: 36.6 us -> 35.2 us (0.962)
  local copies, waits for them, and re-layouts: 2.58 us -> 0 us
  Pallas kernels: 33.1 us -> 34.4 us
    unnamed x2 -> x0, local copies, waits for them, and re-layouts: 2.58 us -> none
    pallas_call x0 -> x1, Pallas kernels: none -> 1.32 us  [local(): pl.pallas_call(finish, name='finish', out_shape=(jax.ShapeDtypeStruct((1,...]
where the time goes in v2:
time: 35.2 us; the launch traced here: 35 us
  Pallas kernels  34.4 us (98%)
  between operations  0.64 us (2%)
    pallas_call x1, Pallas kernels, local(): pl.pallas_call(kernel, name='influence', out_shape=(jax.ShapeDtypeStruct(...  33 us
    pallas_call x1, Pallas kernels, local(): pl.pallas_call(finish, name='finish', out_shape=(jax.ShapeDtypeStruct((1,...  1.32 us

profile of v2, /device:TPU:1, one launch (start us, length us, event | category | flops | bytes accessed | tf_op | source)
XLA Modules:
  0.0 35.0 jit_solution(3451337337444413684)
XLA Ops:
  0.6 33.0 %influence.1 = (bf16[32,128]{1,0:T(8,128)(2,1)}, f32[8,128]{1,0:T(8,128)}) custom-call(bf16[8,128,1792]{2,1,0:T(8,128)(2,1)} %hidden.1, bf16[8,128,512]{2,1,0:T(8,128)(2,1)} %grads.1, bf16[64,1792]{1,0:T(8,128)(2,1)} %bitcast.2, bf16[64,512]{1,0:T(8,128)(2,1)} %bitcast.3, bf16[16,4096]{1,0:T(8,128)(2,1)} %queries.1), custom_call_target="tpu_custom_call" | custom-call | tf_op jit(solution)/shard_map/influence/pallas_call | solution.py:213
  33.7 1.3 %finish.1 = (bf16[1,4096]{1,0:T(2,128)(2,1)}, f32[1,1024]{1,0:T(1,128)}) custom-call(bf16[32,128]{1,0:T(8,128)(2,1)} %get-tuple-element.4.tg, f32[8,128]{1,0:T(8,128)} %get-tuple-element.5.part), custom_call_target="tpu_custom_call" | custom-call | tf_op jit(solution)/shard_map/finish/pallas_call | solution.py:241

commit v3 on v2

--- a/solution.py
+++ b/solution.py
@@ -37,6 +37,10 @@
 
 def nt(a, b):
     return lax.dot_general(a, b, (((1,), (1,)), ((), ())), preferred_element_type=F32)
+
+
+def arrived(buffer, semaphore):
+    pltpu.make_async_copy(buffer, buffer, semaphore).wait()
 
 
 def kernel(
@@ -46,10 +50,10 @@
     t_send, t_recv, tg_send, tg_recv, q_buf, s_send, s_recv,
     h_sem, g_sem, w_sem,
     part_ssem, part_rsem, t_ssem, t_rsem, tg_ssem, tg_rsem,
-    q_ssem, q_rsem, far_ssem, far_rsem, sib_ssem, fwd_ssem, s_ssem, s_rsem,
+    q_ssem, q_rsem, far_ssem, far_rsem, sib_ssem, fwd_ssem, s_ssem, s_rsem, direct_ssem, late_ready,
 ):
     me = position()
-    tensor = lax.axis_index("tensor")
+    tensor, z, core = lax.axis_index("tensor"), me["z"], me["core"]
 
     loads = [
         pltpu.make_async_copy(w_out, wout_raw, w_sem.at[0]),
@@ -68,12 +72,32 @@
             c.start()
         reads.append(pair)
 
+    late = z >= 8
     barrier = pltpu.get_barrier_semaphore()
+
+    def say(semaphore, device):
+        pl.semaphore_signal(semaphore, inc=1, device_id=device, device_id_type=MESH)
+
+    def when(condition, action):
+        pl.when(condition)(action)
+
+    def to_line(semaphore, d):
+        for c in (0, 1):
+            say(semaphore, at(dict(me, core=c), z=d))
+
+    for far in range(8, 16):
+        window = jnp.logical_or(far - z <= 4, far - z >= 12)
+        when(jnp.logical_and(jnp.logical_not(late), jnp.logical_or(core == 1, window)), functools.partial(to_line, barrier, far - z))
     for off in PLANE[:-1]:
-        pl.semaphore_signal(barrier, inc=1, device_id=in_plane(me, off), device_id_type=MESH)
+        say(barrier, in_plane(me, off))
+    for d in (7, 6, 5):
+        when(z + d < 8, functools.partial(to_line, barrier, d))
     for d in (4, -4, 3, -3, 2, -2, 1, -1):
-        for c in (0, 1):
-            pl.semaphore_signal(barrier, inc=1, device_id=at(me, z=d, core=c), device_id_type=MESH)
+        when((z + d) // 8 == z // 8, functools.partial(to_line, barrier, d))
+    place = lax.rem(z, 8)
+    same = jnp.minimum(place, 4) + jnp.minimum(7 - place, 4)
+    close = jnp.where(z < 12, 12 - z, z - 11)
+    expected = 31 + 2 * same + jnp.where(late, close + 8, 2 * jnp.maximum(z - 4, 0))
 
     loads[0].wait()
     for j in range(4):
@@ -93,7 +117,28 @@
             part_send[4 * k + j, 0:64, :] = a[:, 128 * j : 128 * j + 128]
             part_send[4 * k + j, 64:128, :] = b[:, 128 * j : 128 * j + 128]
 
-    pl.semaphore_wait(barrier, 47)
+    pl.semaphore_wait(barrier, expected)
+
+    half = z // 8
+    slot = place * 2 + core
+    mine = queries.at[:, pl.ds(pl.multiple_of(tensor * 512, 512), 512)]
+
+    def near(d, ssem=q_ssem, rsem=q_rsem):
+        if isinstance(d, int) and abs(d) == 4:
+            ssem, rsem = far_ssem, far_rsem
+        return pltpu.make_async_remote_copy(
+            mine, q_buf.at[slot], ssem, rsem, device_id=at(dict(me, core=half), z=d), device_id_type=MESH
+        )
+
+    relay = lax.rem(z + 4, 8)
+    when(late, lambda: near(16 + relay - z, far_ssem, far_rsem).start())
+    high, low = jnp.logical_and(late, z >= 12), jnp.logical_and(late, z < 12)
+    directs = []
+    for k in range(8):
+        goes = jnp.logical_and(relay != k, late if k < 2 else high if k < 4 else low)
+        directs.append((goes, near(16 + k - z, direct_ssem)))
+        when(goes, lambda k=k: directs[k][1].start())
+
     for k, (y, h) in enumerate(TENSOR):
         example = lax.rem(me["y"] + y + 2, 4) * 2 + lax.rem(me["x_hi"] + h + 1, 2)
         if k == 7:
@@ -104,45 +149,19 @@
             device_id=at(me, y=y, x_hi=h), device_id_type=MESH,
         ).start()
 
-    half = me["z"] // 8
-    slot = lax.rem(me["z"], 8) * 2 + me["core"]
-    mine = queries.at[:, pl.ds(pl.multiple_of(tensor * 512, 512), 512)]
-
-    def near(d, ssem, rsem):
-        target = at(dict(me, core=half), z=d)
-        return pltpu.make_async_remote_copy(
-            mine, q_buf.at[slot], ssem, rsem, device_id=target, device_id_type=MESH
-        )
-
-    for d in (4, -4):
-        near(d, far_ssem, far_rsem).start()
-    for d in (3, -3, 2, -2, 1, -1):
-        near(d, q_ssem, q_rsem).start()
-    sibling = near(0, sib_ssem, q_rsem)
+    for d in (-4, 4, -3, 3, -2, 2, -1, 1):
+        when((z + d) // 8 == half, lambda d=d: near(d).start())
+    sibling = near(0, sib_ssem)
     own = pltpu.make_async_copy(mine, q_buf.at[slot], q_rsem)
-
-    @pl.when(half == me["core"])
-    def _():
-        own.start()
-
-    @pl.when(half != me["core"])
-    def _():
-        sibling.start()
-
-    back = lax.rem(me["z"] + 12, 16)
-    up = (back // 8) == me["core"]
-    sign = jnp.where(up, 1, -1)
-    source = lax.rem(me["z"] - 4 * sign + 16, 16)
-    first = lax.rem(source, 8) * 2
-    pltpu.make_async_copy(q_buf.at[pl.ds(0, 2)], q_buf.at[pl.ds(0, 2)], far_rsem).wait()
-    for c, d in ((0, 3), (1, 3), (0, 2), (1, 2), (0, 1), (1, 1), (None, 4)):
-        block = first + (jnp.where(up, 0, 1) if c is None else c)
-        pltpu.make_async_remote_copy(
-            q_buf.at[block], q_buf.at[block], fwd_ssem, q_rsem,
-            device_id=at(me, z=sign * d), device_id_type=MESH,
-        ).start()
-
-    pltpu.make_async_copy(part_recv, part_recv, part_rsem).wait()
+    when(half == core, lambda: own.start())
+    when(half != core, lambda: sibling.start())
+    for d in (4, 3, 2, 1):
+        when(jnp.logical_and(late, jnp.logical_and(z - d < 8, z - d >= 4)), functools.partial(to_line, late_ready, -d))
+        when(z + d >= 16, functools.partial(to_line, late_ready, d))
+    for d in (7, 6, 5):
+        when(jnp.logical_and(z < 8, z - d >= 0), functools.partial(to_line, late_ready, -d))
+
+    arrived(part_recv, part_rsem)
     total = part_recv[0].astype(F32)
     for k in range(1, 8):
         total += part_recv[k].astype(F32)
@@ -167,14 +186,44 @@
     )
     whole.start()
 
-    pltpu.make_async_copy(q_buf.at[pl.ds(0, 14)], q_buf.at[pl.ds(0, 14)], q_rsem).wait()
-    pltpu.make_async_copy(t_recv, t_recv, t_rsem).wait()
+    answers = jnp.where(z < 4, 4 - z, z - 3) + jnp.maximum(3 - z, 0)
+    when(jnp.logical_not(late), lambda: pl.semaphore_wait(late_ready, 2 * answers))
+    for d in (4, 3, 2, 1):
+        when(z - d < 0, lambda d=d: near(-d).start())
+        when(jnp.logical_and(jnp.logical_not(late), z + d >= 8), lambda d=d: near(d).start())
+
+    up = (lax.rem(z + 12, 16) // 8) == core
+    sign = jnp.where(up, 1, -1)
+    first = lax.rem(lax.rem(z - 4 * sign + 16, 16), 8) * 2
+    arrived(q_buf.at[pl.ds(0, 2)], far_rsem)
+    wanted = []
+    for c, d in ((None, 4), (0, 3), (1, 3), (0, 2), (1, 2), (0, 1), (1, 1)):
+        block = first + (jnp.where(up, 0, 1) if c is None else c)
+        goal = lax.rem(z + sign * d + 16, 16)
+        copy = pltpu.make_async_remote_copy(
+            q_buf.at[block], q_buf.at[block], fwd_ssem, q_rsem,
+            device_id=at(me, z=sign * d), device_id_type=MESH,
+        )
+        wanted.append((jnp.logical_or(core == 0, goal >= 8), copy))
+        when(wanted[-1][0], lambda copy=copy: copy.start())
+    holds = jnp.logical_and(core == 1, jnp.logical_not(late))
+    for goal in (2, 3, 4, 5, 6, 7):
+        for c in (0, 1):
+            copy = pltpu.make_async_remote_copy(
+                q_buf.at[first + c], q_buf.at[first + c], fwd_ssem, q_rsem,
+                device_id=at(me, z=goal - z + 16), device_id_type=MESH,
+            )
+            wanted.append((jnp.logical_and(holds, z >= 4 if goal < 4 else z < 4), copy))
+            when(wanted[-1][0], lambda copy=copy: copy.start())
+
+    arrived(q_buf.at[pl.ds(0, 14)], q_rsem)
+    arrived(t_recv, t_rsem)
     x = jnp.concatenate([t_recv[:, k, :] for k in range(4)], axis=1).astype(BF16)
     part = nt(x, q_buf[...].reshape(256, 512)) * (1.0 / 64)
     for k in range(2):
         s_send[:, k, :] = part[:, 128 * k : 128 * k + 128]
-    place = (me["x_lo"] * 2 + me["core"]) * 8 + tensor
-    for s, off in enumerate(PLANE):
+    place = (me["x_lo"] * 2 + core) * 8 + tensor
+    for s, off in reversed(list(enumerate(PLANE))):
         if off == OPPOSITE:
             pltpu.make_async_copy(s_send.at[s], s_recv.at[place], s_rsem).start()
             continue
@@ -183,24 +232,25 @@
             s_send.at[s], s_recv.at[place], s_ssem, s_rsem, device_id=in_plane(me, back), device_id_type=MESH
         ).start()
 
-    pltpu.make_async_copy(part_send.at[pl.ds(0, 7)], part_send.at[pl.ds(0, 7)], part_ssem).wait()
-    pltpu.make_async_copy(t_recv.at[pl.ds(0, 31)], t_recv.at[pl.ds(0, 31)], t_ssem).wait()
+    arrived(part_send.at[pl.ds(0, 7)], part_ssem)
+    arrived(t_recv.at[pl.ds(0, 31)], t_ssem)
     whole.wait_send()
-    pltpu.make_async_copy(q_buf.at[pl.ds(0, 2)], q_buf.at[pl.ds(0, 2)], far_ssem).wait()
-    pltpu.make_async_copy(q_buf.at[pl.ds(0, 6)], q_buf.at[pl.ds(0, 6)], q_ssem).wait()
-    pltpu.make_async_copy(q_buf.at[pl.ds(0, 7)], q_buf.at[pl.ds(0, 7)], fwd_ssem).wait()
-
-    @pl.when(half != me["core"])
-    def _():
-        sibling.wait_send()
+    arrived(q_buf.at[pl.ds(0, 2)], far_ssem)
+    for goes, copy in directs:
+        when(goes, lambda copy=copy: copy.wait_send())
+    for d in (3, -3, 2, -2, 1, -1):
+        when(jnp.logical_or(jnp.logical_not(late), (z + d) // 8 == half), lambda d=d: near(d).wait_send())
+    for condition, copy in wanted:
+        when(condition, lambda copy=copy: copy.wait_send())
+    when(half != core, lambda: sibling.wait_send())
 
     whole.wait_recv()
     tg_out[...] = tg_recv[...]
 
-    pltpu.make_async_copy(s_recv, s_recv, s_rsem).wait()
+    arrived(s_recv, s_rsem)
     for w in range(4):
         scores_out[2 * w : 2 * w + 2, :] = jnp.sum(s_recv[8 * w : 8 * w + 8], axis=0)
-    pltpu.make_async_copy(s_recv.at[pl.ds(0, 31)], s_recv.at[pl.ds(0, 31)], s_ssem).wait()
+    arrived(s_recv.at[pl.ds(0, 31)], s_ssem)
 
 
 def finish(tg, part, tg_out, scores_out):
@@ -233,7 +283,7 @@
             pltpu.VMEM((32, 2, 128), F32),
             pltpu.VMEM((32, 2, 128), F32),
             dma((2,)), dma((2,)), dma((2,)),
-        ] + [dma] * 14,
+        ] + [dma] * 15 + [pltpu.SemaphoreType.REGULAR],
         compiler_params=pltpu.CompilerParams(
             collective_id=0, has_side_effects=True, vmem_limit_bytes=56 * 1024 * 1024
         ),

time: 35.2 us -> 34.2 us (0.972)
  Pallas kernels: 34.4 us -> 33.4 us
    pallas_call x1, Pallas kernels: 33 us -> 32.1 us  [local(): pl.pallas_call(kernel, name='influence', out_shape=(jax.ShapeDtypeStruct(...]
where the time goes in v3:
time: 34.2 us; the launch traced here: 34 us
  Pallas kernels  33.4 us (98%)
  between operations  0.64 us (2%)
    pallas_call x1, Pallas kernels, local(): pl.pallas_call(kernel, name='influence', out_shape=(jax.ShapeDtypeStruct(...  32.1 us
    pallas_call x1, Pallas kernels, local(): pl.pallas_call(finish, name='finish', out_shape=(jax.ShapeDtypeStruct((1,...  1.32 us

profile of v3, /device:TPU:1, one launch (start us, length us, event | category | flops | bytes accessed | tf_op | source)
XLA Modules:
  0.0 34.0 jit_solution(7737352701373358191)
XLA Ops:
  0.6 32.1 %influence.1 = (bf16[32,128]{1,0:T(8,128)(2,1)}, f32[8,128]{1,0:T(8,128)}) custom-call(bf16[8,128,1792]{2,1,0:T(8,128)(2,1)} %hidden.1, bf16[8,128,512]{2,1,0:T(8,128)(2,1)} %grads.1, bf16[64,1792]{1,0:T(8,128)(2,1)} %bitcast.2, bf16[64,512]{1,0:T(8,128)(2,1)} %bitcast.3, bf16[16,4096]{1,0:T(8,128)(2,1)} %queries.1), custom_call_target="tpu_custom_call" | custom-call | tf_op jit(solution)/shard_map/influence/pallas_call | solution.py:263
  32.7 1.3 %finish.1 = (bf16[1,4096]{1,0:T(2,128)(2,1)}, f32[1,1024]{1,0:T(1,128)}) custom-call(bf16[32,128]{1,0:T(8,128)(2,1)} %get-tuple-element.4.tg, f32[8,128]{1,0:T(8,128)} %get-tuple-element.5.part), custom_call_target="tpu_custom_call" | custom-call | tf_op jit(solution)/shard_map/finish/pallas_call | solution.py:291

commit v4 on v3

--- a/solution.py
+++ b/solution.py
@@ -11,8 +11,17 @@
 SIZES = dict(x_lo=2, z=16, core=2, y=4, x_hi=2)
 F32, BF16 = jnp.float32, jnp.bfloat16
 
-TENSOR = [(2, 1), (1, 1), (3, 1), (2, 0), (0, 1), (1, 0), (3, 0), (0, 0)]
-PLANE = [(y, h, l, c) for y, h in TENSOR for l in (1, 0) for c in (1, 0)]
+
+def hops(offset):
+    y, x_hi, x_lo, _ = offset
+    return min(y, 4 - y) + (1 if x_lo else 2 * x_hi)
+
+
+PLANE = sorted(
+    ((y, h, l, c) for y in range(4) for h in range(2) for l in range(2) for c in range(2)),
+    key=lambda o: (-hops(o), o == (0, 0, 0, 0), o),
+)
+TENSOR = [o for o in PLANE if o[2:] == (0, 0)]
 OPPOSITE = (2, 1, 0, 0)
 
 
@@ -31,8 +40,14 @@
     }
 
 
-def in_plane(place, offset):
-    return at(place, **dict(zip(("y", "x_hi", "x_lo", "core"), offset)))
+def plane_map(place):
+    dp = {(l, c): at(place, x_lo=l, core=c)["dp"] for l in range(2) for c in range(2)}
+    tensor = {(y, h): at(place, y=y, x_hi=h)["tensor"] for y in range(4) for h in range(2)}
+    return {o: {"dp": dp[o[2:]], "tensor": tensor[o[:2]]} for o in PLANE}
+
+
+def difference(a, b):
+    return tuple((p - q) % n for p, q, n in zip(a, b, (4, 2, 2, 2)))
 
 
 def nt(a, b):
@@ -47,17 +62,21 @@
     hidden, grads, w_in, w_out, queries, tg_out, scores_out,
     h_buf, g_buf, win_buf, wout_raw, wout_f32, wout_buf,
     part_send, part_recv,
-    t_send, t_recv, tg_send, tg_recv, q_buf, s_send, s_recv,
+    t_send, t_recv, tg_send, tg_recv, q_buf, mine, x_buf, s_send, s_recv,
     h_sem, g_sem, w_sem,
     part_ssem, part_rsem, t_ssem, t_rsem, tg_ssem, tg_rsem,
     q_ssem, q_rsem, far_ssem, far_rsem, sib_ssem, fwd_ssem, s_ssem, s_rsem, direct_ssem, late_ready,
 ):
     me = position()
     tensor, z, core = lax.axis_index("tensor"), me["z"], me["core"]
+    device = plane_map(me)
 
     loads = [
         pltpu.make_async_copy(w_out, wout_raw, w_sem.at[0]),
         pltpu.make_async_copy(w_in, win_buf, w_sem.at[1]),
+        pltpu.make_async_copy(
+            queries.at[:, pl.ds(pl.multiple_of(tensor * 512, 512), 512)], mine, w_sem.at[2]
+        ),
     ]
     for c in loads:
         c.start()
@@ -89,7 +108,7 @@
         window = jnp.logical_or(far - z <= 4, far - z >= 12)
         when(jnp.logical_and(jnp.logical_not(late), jnp.logical_or(core == 1, window)), functools.partial(to_line, barrier, far - z))
     for off in PLANE[:-1]:
-        say(barrier, in_plane(me, off))
+        say(barrier, device[off])
     for d in (7, 6, 5):
         when(z + d < 8, functools.partial(to_line, barrier, d))
     for d in (4, -4, 3, -3, 2, -2, 1, -1):
@@ -121,7 +140,7 @@
 
     half = z // 8
     slot = place * 2 + core
-    mine = queries.at[:, pl.ds(pl.multiple_of(tensor * 512, 512), 512)]
+    loads[2].wait()
 
     def near(d, ssem=q_ssem, rsem=q_rsem):
         if isinstance(d, int) and abs(d) == 4:
@@ -139,14 +158,14 @@
         directs.append((goes, near(16 + k - z, direct_ssem)))
         when(goes, lambda k=k: directs[k][1].start())
 
-    for k, (y, h) in enumerate(TENSOR):
-        example = lax.rem(me["y"] + y + 2, 4) * 2 + lax.rem(me["x_hi"] + h + 1, 2)
+    for k, off in enumerate(TENSOR):
+        example = device[difference(off, OPPOSITE)]["tensor"]
         if k == 7:
             pltpu.make_async_copy(part_send.at[example], part_recv.at[k], part_rsem).start()
             continue
         pltpu.make_async_remote_copy(
             part_send.at[example], part_recv.at[k], part_ssem, part_rsem,
-            device_id=at(me, y=y, x_hi=h), device_id_type=MESH,
+            device_id=device[off], device_id_type=MESH,
         ).start()
 
     for d in (-4, 4, -3, 3, -2, 2, -1, 1):
@@ -176,13 +195,13 @@
         t_send[k] = wide[4 * k : 4 * k + 4]
 
     for s, off in enumerate(PLANE[:-1]):
-        target = in_plane(me, off)
+        target = device[off]
         pltpu.make_async_remote_copy(
             t_send.at[target["tensor"]], t_recv.at[s], t_ssem, t_rsem, device_id=target, device_id_type=MESH
         ).start()
     pltpu.make_async_copy(t_send.at[tensor], t_recv.at[31], t_rsem).start()
     whole = pltpu.make_async_remote_copy(
-        tg_send, tg_recv, tg_ssem, tg_rsem, device_id=in_plane(me, OPPOSITE), device_id_type=MESH
+        tg_send, tg_recv, tg_ssem, tg_rsem, device_id=device[OPPOSITE], device_id_type=MESH
     )
     whole.start()
 
@@ -216,20 +235,20 @@
             wanted.append((jnp.logical_and(holds, z >= 4 if goal < 4 else z < 4), copy))
             when(wanted[-1][0], lambda copy=copy: copy.start())
 
+    arrived(t_recv, t_rsem)
+    for k in range(4):
+        x_buf[:, 128 * k : 128 * k + 128] = t_recv[:, k, :].astype(BF16)
     arrived(q_buf.at[pl.ds(0, 14)], q_rsem)
-    arrived(t_recv, t_rsem)
-    x = jnp.concatenate([t_recv[:, k, :] for k in range(4)], axis=1).astype(BF16)
-    part = nt(x, q_buf[...].reshape(256, 512)) * (1.0 / 64)
+    part = nt(x_buf[...], q_buf[...].reshape(256, 512)) * (1.0 / 64)
     for k in range(2):
         s_send[:, k, :] = part[:, 128 * k : 128 * k + 128]
     place = (me["x_lo"] * 2 + core) * 8 + tensor
-    for s, off in reversed(list(enumerate(PLANE))):
+    for s, off in sorted(enumerate(PLANE), key=lambda p: -hops(difference(OPPOSITE, p[1]))):
         if off == OPPOSITE:
             pltpu.make_async_copy(s_send.at[s], s_recv.at[place], s_rsem).start()
             continue
-        back = tuple(o - p for o, p in zip(OPPOSITE, off))
         pltpu.make_async_remote_copy(
-            s_send.at[s], s_recv.at[place], s_ssem, s_rsem, device_id=in_plane(me, back), device_id_type=MESH
+            s_send.at[s], s_recv.at[place], s_ssem, s_rsem, device_id=device[difference(OPPOSITE, off)], device_id_type=MESH
         ).start()
 
     arrived(part_send.at[pl.ds(0, 7)], part_ssem)
@@ -280,18 +299,23 @@
             pltpu.VMEM((32, 128), BF16),
             pltpu.VMEM((32, 128), BF16),
             pltpu.VMEM((16, 16, 512), BF16),
+            pltpu.VMEM((16, 512), BF16),
+            pltpu.VMEM((32, 512), BF16),
             pltpu.VMEM((32, 2, 128), F32),
             pltpu.VMEM((32, 2, 128), F32),
-            dma((2,)), dma((2,)), dma((2,)),
+            dma((2,)), dma((2,)), dma((3,)),
         ] + [dma] * 15 + [pltpu.SemaphoreType.REGULAR],
         compiler_params=pltpu.CompilerParams(
-            collective_id=0, has_side_effects=True, vmem_limit_bytes=56 * 1024 * 1024
+            collective_id=0, has_side_effects=True, vmem_limit_bytes=539 * 1024 * 1024 // 10
         ),
     )(hidden_acts, out_grads, proj_in.T, proj_out.T, queries)
     return pl.pallas_call(
         finish,
         name="finish",
         out_shape=(jax.ShapeDtypeStruct((1, 4096), BF16), jax.ShapeDtypeStruct((1, 1024), F32)),
+        in_specs=[pl.BlockSpec(memory_space=pltpu.VMEM)] * 2,
+        out_specs=(pl.BlockSpec(memory_space=pltpu.VMEM),) * 2,
+        compiler_params=pltpu.CompilerParams(vmem_limit_bytes=1024 * 1024),
     )(tg, scores)
 
 

time: 34.2 us -> 32.5 us (0.950)
  Pallas kernels: 33.4 us -> 31.7 us
    pallas_call x1, Pallas kernels: 32.1 us -> 31.1 us  [local(): pl.pallas_call(kernel, name='influence', out_shape=(jax.ShapeDtypeStruct(...]
    pallas_call x1, Pallas kernels: 1.32 us -> 0.62 us  [local(): pl.pallas_call(finish, name='finish', out_shape=(jax.ShapeDtypeStruct((1,...]
where the time goes in v4:
time: 32.5 us; the launch traced here: 32.4 us
  Pallas kernels  31.7 us (98%)
  between operations  0.64 us (2%)
    pallas_call x1, Pallas kernels, local(): pl.pallas_call(kernel, name='influence', out_shape=(jax.ShapeDtypeStruct(...  31.1 us

profile of v4, /device:TPU:1, one launch (start us, length us, event | category | flops | bytes accessed | tf_op | source)
XLA Modules:
  0.0 32.4 jit_solution(4004487203526945514)
XLA Ops:
  0.6 31.1 %influence.1 = (bf16[32,128]{1,0:T(8,128)(2,1)S(1)}, f32[8,128]{1,0:T(8,128)S(1)}) custom-call(bf16[8,128,1792]{2,1,0:T(8,128)(2,1)} %hidden.1, bf16[8,128,512]{2,1,0:T(8,128)(2,1)} %grads.1, bf16[64,1792]{1,0:T(8,128)(2,1)} %bitcast.2, bf16[64,512]{1,0:T(8,128)(2,1)} %bitcast.3, bf16[16,4096]{1,0:T(8,128)(2,1)} %queries.1), custom_call_target="tpu_custom_call" | custom-call | tf_op jit(solution)/shard_map/influence/pallas_call | solution.py:282
  31.7 0.6 %finish.1 = (bf16[1,4096]{1,0:T(2,128)(2,1)}, f32[1,1024]{1,0:T(1,128)}) custom-call(bf16[32,128]{1,0:T(8,128)(2,1)S(1)} %get-tuple-element.4.tg, f32[8,128]{1,0:T(8,128)S(1)} %get-tuple-element.5.part), custom_call_target="tpu_custom_call" | custom-call | tf_op jit(solution)/shard_map/finish/pallas_call | solution.py:312

commit v5 on v4

--- a/solution.py
+++ b/solution.py
@@ -104,15 +104,17 @@
         for c in (0, 1):
             say(semaphore, at(dict(me, core=c), z=d))
 
-    for far in range(8, 16):
-        window = jnp.logical_or(far - z <= 4, far - z >= 12)
-        when(jnp.logical_and(jnp.logical_not(late), jnp.logical_or(core == 1, window)), functools.partial(to_line, barrier, far - z))
+    def to_second_half():
+        for far in range(8, 16):
+            window = jnp.logical_or(far - z <= 4, far - z >= 12)
+            when(jnp.logical_or(core == 1, window), functools.partial(to_line, barrier, far - z))
+
+    when(jnp.logical_not(late), to_second_half)
     for off in PLANE[:-1]:
         say(barrier, device[off])
-    for d in (7, 6, 5):
-        when(z + d < 8, functools.partial(to_line, barrier, d))
     for d in (4, -4, 3, -3, 2, -2, 1, -1):
         when((z + d) // 8 == z // 8, functools.partial(to_line, barrier, d))
+    when(z < 3, lambda: [when(z + d < 8, functools.partial(to_line, barrier, d)) for d in (7, 6, 5)] and None)
     place = lax.rem(z, 8)
     same = jnp.minimum(place, 4) + jnp.minimum(7 - place, 4)
     close = jnp.where(z < 12, 12 - z, z - 11)
@@ -150,13 +152,38 @@
         )
 
     relay = lax.rem(z + 4, 8)
-    when(late, lambda: near(16 + relay - z, far_ssem, far_rsem).start())
-    high, low = jnp.logical_and(late, z >= 12), jnp.logical_and(late, z < 12)
-    directs = []
-    for k in range(8):
-        goes = jnp.logical_and(relay != k, late if k < 2 else high if k < 4 else low)
-        directs.append((goes, near(16 + k - z, direct_ssem)))
-        when(goes, lambda k=k: directs[k][1].start())
+    high, low = z >= 12, jnp.logical_and(late, z < 12)
+
+    def straight(goal):
+        return near(16 + goal - z, direct_ssem)
+
+    def from_second_half():
+        @pl.when(z >= 12)
+        def _():
+            near(16 + relay - z, far_ssem, far_rsem).start()
+            for goal in range(4):
+                when(relay != goal, lambda goal=goal: straight(goal).start())
+
+        @pl.when(z < 12)
+        def _():
+            near(16 + relay - z, far_ssem, far_rsem).start()
+            for goal in (0, 1, 2):
+                straight(goal).start()
+            for j in (1, 2, 3):
+                straight(4 + lax.rem(relay + j, 4)).start()
+
+        for d in (4, 3, 2, 1):
+            when(jnp.logical_and(z - d < 8, z < 12), functools.partial(to_line, late_ready, -d))
+            when(z + d >= 16, functools.partial(to_line, late_ready, d))
+
+    when(late, from_second_half)
+
+    def to_first_three():
+        for d in (7, 6, 5):
+            when(z - d >= 0, functools.partial(to_line, late_ready, -d))
+            when(z - d >= 0, lambda d=d: near(-d, direct_ssem).start())
+
+    distant = jnp.logical_and(z >= 5, z < 8)
 
     for k, off in enumerate(TENSOR):
         example = device[difference(off, OPPOSITE)]["tensor"]
@@ -170,16 +197,11 @@
 
     for d in (-4, 4, -3, 3, -2, 2, -1, 1):
         when((z + d) // 8 == half, lambda d=d: near(d).start())
+    when(distant, to_first_three)
     sibling = near(0, sib_ssem)
     own = pltpu.make_async_copy(mine, q_buf.at[slot], q_rsem)
     when(half == core, lambda: own.start())
     when(half != core, lambda: sibling.start())
-    for d in (4, 3, 2, 1):
-        when(jnp.logical_and(late, jnp.logical_and(z - d < 8, z - d >= 4)), functools.partial(to_line, late_ready, -d))
-        when(z + d >= 16, functools.partial(to_line, late_ready, d))
-    for d in (7, 6, 5):
-        when(jnp.logical_and(z < 8, z - d >= 0), functools.partial(to_line, late_ready, -d))
-
     arrived(part_recv, part_rsem)
     total = part_recv[0].astype(F32)
     for k in range(1, 8):
@@ -205,35 +227,52 @@
     )
     whole.start()
 
-    answers = jnp.where(z < 4, 4 - z, z - 3) + jnp.maximum(3 - z, 0)
-    when(jnp.logical_not(late), lambda: pl.semaphore_wait(late_ready, 2 * answers))
-    for d in (4, 3, 2, 1):
-        when(z - d < 0, lambda d=d: near(-d).start())
-        when(jnp.logical_and(jnp.logical_not(late), z + d >= 8), lambda d=d: near(d).start())
-
     up = (lax.rem(z + 12, 16) // 8) == core
     sign = jnp.where(up, 1, -1)
     first = lax.rem(lax.rem(z - 4 * sign + 16, 16), 8) * 2
-    arrived(q_buf.at[pl.ds(0, 2)], far_rsem)
+    holds = jnp.logical_and(core == 1, jnp.logical_not(late))
+    early = jnp.logical_and(holds, z >= 4)
+
+    def pass_on(block, target):
+        return pltpu.make_async_remote_copy(
+            q_buf.at[block], q_buf.at[block], fwd_ssem, q_rsem, device_id=target, device_id_type=MESH
+        )
+
+    @pl.when(early)
+    def _():
+        arrived(q_buf.at[pl.ds(0, 2)], far_rsem)
+        for goal in (3,):
+            for c in (0, 1):
+                pass_on(first + c, at(me, z=goal - z + 16)).start()
+
+    @pl.when(jnp.logical_not(late))
+    def _():
+        answers = jnp.where(z < 4, 4 - z, z - 3) + jnp.maximum(3 - z, 0)
+        pl.semaphore_wait(late_ready, 2 * answers)
+        for d in (4, 3, 2, 1):
+            when(z - d < 0, lambda d=d: near(-d).start())
+            when(z + d >= 8, lambda d=d: near(d).start())
+
+    lower = jnp.logical_and(holds, z < 4)
+
+    @pl.when(lower)
+    def _():
+        arrived(q_buf.at[pl.ds(0, 2)], far_rsem)
+        for goal in (4, 5, 6, 7):
+            for c in (0, 1):
+                pass_on(first + c, at(me, z=goal - z + 16)).start()
+
     wanted = []
     for c, d in ((None, 4), (0, 3), (1, 3), (0, 2), (1, 2), (0, 1), (1, 1)):
         block = first + (jnp.where(up, 0, 1) if c is None else c)
         goal = lax.rem(z + sign * d + 16, 16)
-        copy = pltpu.make_async_remote_copy(
-            q_buf.at[block], q_buf.at[block], fwd_ssem, q_rsem,
-            device_id=at(me, z=sign * d), device_id_type=MESH,
-        )
-        wanted.append((jnp.logical_or(core == 0, goal >= 8), copy))
-        when(wanted[-1][0], lambda copy=copy: copy.start())
-    holds = jnp.logical_and(core == 1, jnp.logical_not(late))
-    for goal in (2, 3, 4, 5, 6, 7):
-        for c in (0, 1):
-            copy = pltpu.make_async_remote_copy(
-                q_buf.at[first + c], q_buf.at[first + c], fwd_ssem, q_rsem,
-                device_id=at(me, z=goal - z + 16), device_id_type=MESH,
-            )
-            wanted.append((jnp.logical_and(holds, z >= 4 if goal < 4 else z < 4), copy))
-            when(wanted[-1][0], lambda copy=copy: copy.start())
+        wanted.append((jnp.logical_or(goal >= 8, jnp.logical_and(core == 0, z >= 4)), pass_on(block, at(me, z=sign * d))))
+
+    @pl.when(jnp.logical_not(holds))
+    def _():
+        arrived(q_buf.at[pl.ds(0, 2)], far_rsem)
+        for condition, copy in wanted:
+            when(condition, lambda copy=copy: copy.start())
 
     arrived(t_recv, t_rsem)
     for k in range(4):
@@ -255,12 +294,16 @@
     arrived(t_recv.at[pl.ds(0, 31)], t_ssem)
     whole.wait_send()
     arrived(q_buf.at[pl.ds(0, 2)], far_ssem)
-    for goes, copy in directs:
-        when(goes, lambda copy=copy: copy.wait_send())
+    when(high, lambda: arrived(q_buf.at[pl.ds(0, 3)], direct_ssem))
+    when(low, lambda: arrived(q_buf.at[pl.ds(0, 6)], direct_ssem))
+    for d in (7, 6, 5):
+        when(jnp.logical_and(distant, z - d >= 0), lambda d=d: near(-d, direct_ssem).wait_send())
     for d in (3, -3, 2, -2, 1, -1):
         when(jnp.logical_or(jnp.logical_not(late), (z + d) // 8 == half), lambda d=d: near(d).wait_send())
+    when(early, lambda: arrived(q_buf.at[pl.ds(0, 2)], fwd_ssem))
+    when(lower, lambda: arrived(q_buf.at[pl.ds(0, 8)], fwd_ssem))
     for condition, copy in wanted:
-        when(condition, lambda copy=copy: copy.wait_send())
+        when(jnp.logical_and(jnp.logical_not(holds), condition), lambda copy=copy: copy.wait_send())
     when(half != core, lambda: sibling.wait_send())
 
     whole.wait_recv()

time: 32.5 us -> 31.9 us (0.982)
  Pallas kernels: 31.7 us -> 31.2 us
    pallas_call x1, Pallas kernels: 31.1 us -> 30.5 us  [local(): pl.pallas_call(kernel, name='influence', out_shape=(jax.ShapeDtypeStruct(...]
where the time goes in v5:
time: 31.9 us; the launch traced here: 31.8 us
  Pallas kernels  31.2 us (98%)
  between operations  0.64 us (2%)
    pallas_call x1, Pallas kernels, local(): pl.pallas_call(kernel, name='influence', out_shape=(jax.ShapeDtypeStruct(...  30.5 us

profile of v5, /device:TPU:1, one launch (start us, length us, event | category | flops | bytes accessed | tf_op | source)
XLA Modules:
  0.0 31.8 jit_solution(2448022884326747311)
XLA Ops:
  0.6 30.5 %influence.1 = (bf16[32,128]{1,0:T(8,128)(2,1)S(1)}, f32[8,128]{1,0:T(8,128)S(1)}) custom-call(bf16[8,128,1792]{2,1,0:T(8,128)(2,1)} %hidden.1, bf16[8,128,512]{2,1,0:T(8,128)(2,1)} %grads.1, bf16[64,1792]{1,0:T(8,128)(2,1)} %bitcast.2, bf16[64,512]{1,0:T(8,128)(2,1)} %bitcast.3, bf16[16,4096]{1,0:T(8,128)(2,1)} %queries.1), custom_call_target="tpu_custom_call" | custom-call | tf_op jit(solution)/shard_map/influence/pallas_call | solution.py:325
  31.2 0.6 %finish.1 = (bf16[1,4096]{1,0:T(2,128)(2,1)}, f32[1,1024]{1,0:T(1,128)}) custom-call(bf16[32,128]{1,0:T(8,128)(2,1)S(1)} %get-tuple-element.4.tg, f32[8,128]{1,0:T(8,128)S(1)} %get-tuple-element.5.part), custom_call_target="tpu_custom_call" | custom-call | tf_op jit(solution)/shard_map/finish/pallas_call | solution.py:355

commit v6 on v5

--- a/solution.py
+++ b/solution.py
@@ -110,9 +110,11 @@
             when(jnp.logical_or(core == 1, window), functools.partial(to_line, barrier, far - z))
 
     when(jnp.logical_not(late), to_second_half)
+    for d in (4, -4, 3, -3):
+        when((z + d) // 8 == z // 8, functools.partial(to_line, barrier, d))
     for off in PLANE[:-1]:
         say(barrier, device[off])
-    for d in (4, -4, 3, -3, 2, -2, 1, -1):
+    for d in (2, -2, 1, -1):
         when((z + d) // 8 == z // 8, functools.partial(to_line, barrier, d))
     when(z < 3, lambda: [when(z + d < 8, functools.partial(to_line, barrier, d)) for d in (7, 6, 5)] and None)
     place = lax.rem(z, 8)
@@ -233,6 +235,8 @@
     holds = jnp.logical_and(core == 1, jnp.logical_not(late))
     early = jnp.logical_and(holds, z >= 4)
 
+    both_cores = pl.ds(first, 2)
+
     def pass_on(block, target):
         return pltpu.make_async_remote_copy(
             q_buf.at[block], q_buf.at[block], fwd_ssem, q_rsem, device_id=target, device_id_type=MESH
@@ -241,9 +245,7 @@
     @pl.when(early)
     def _():
         arrived(q_buf.at[pl.ds(0, 2)], far_rsem)
-        for goal in (3,):
-            for c in (0, 1):
-                pass_on(first + c, at(me, z=goal - z + 16)).start()
+        pass_on(both_cores, at(me, z=3 - z + 16)).start()
 
     @pl.when(jnp.logical_not(late))
     def _():
@@ -259,12 +261,11 @@
     def _():
         arrived(q_buf.at[pl.ds(0, 2)], far_rsem)
         for goal in (4, 5, 6, 7):
-            for c in (0, 1):
-                pass_on(first + c, at(me, z=goal - z + 16)).start()
+            pass_on(both_cores, at(me, z=goal - z + 16)).start()
 
     wanted = []
-    for c, d in ((None, 4), (0, 3), (1, 3), (0, 2), (1, 2), (0, 1), (1, 1)):
-        block = first + (jnp.where(up, 0, 1) if c is None else c)
+    for d in (4, 3, 2, 1):
+        block = first + jnp.where(up, 0, 1) if d == 4 else both_cores
         goal = lax.rem(z + sign * d + 16, 16)
         wanted.append((jnp.logical_or(goal >= 8, jnp.logical_and(core == 0, z >= 4)), pass_on(block, at(me, z=sign * d))))
 

time: 31.9 us -> 31.6 us (level)
  no operation moved by 1% of the time
where the time goes in v6:
time: 31.6 us; the launch traced here: 31.5 us
  Pallas kernels  30.9 us (98%)
  between operations  0.64 us (2%)
    pallas_call x1, Pallas kernels, local(): pl.pallas_call(kernel, name='influence', out_shape=(jax.ShapeDtypeStruct(...  30.2 us

profile of v6, /device:TPU:1, one launch (start us, length us, event | category | flops | bytes accessed | tf_op | source)
XLA Modules:
  0.0 31.5 jit_solution(1224573244193840519)
XLA Ops:
  0.6 30.2 %influence.1 = (bf16[32,128]{1,0:T(8,128)(2,1)S(1)}, f32[8,128]{1,0:T(8,128)S(1)}) custom-call(bf16[8,128,1792]{2,1,0:T(8,128)(2,1)} %hidden.1, bf16[8,128,512]{2,1,0:T(8,128)(2,1)} %grads.1, bf16[64,1792]{1,0:T(8,128)(2,1)} %bitcast.2, bf16[64,512]{1,0:T(8,128)(2,1)} %bitcast.3, bf16[16,4096]{1,0:T(8,128)(2,1)} %queries.1), custom_call_target="tpu_custom_call" | custom-call | tf_op jit(solution)/shard_map/influence/pallas_call | solution.py:326
  30.9 0.6 %finish.1 = (bf16[1,4096]{1,0:T(2,128)(2,1)}, f32[1,1024]{1,0:T(1,128)}) custom-call(bf16[32,128]{1,0:T(8,128)(2,1)S(1)} %get-tuple-element.4.tg, f32[8,128]{1,0:T(8,128)S(1)} %get-tuple-element.5.part), custom_call_target="tpu_custom_call" | custom-call | tf_op jit(solution)/shard_map/finish/pallas_call | solution.py:356

commit v7 on v6

--- a/solution.py
+++ b/solution.py
@@ -279,7 +279,7 @@
     for k in range(4):
         x_buf[:, 128 * k : 128 * k + 128] = t_recv[:, k, :].astype(BF16)
     arrived(q_buf.at[pl.ds(0, 14)], q_rsem)
-    part = nt(x_buf[...], q_buf[...].reshape(256, 512)) * (1.0 / 64)
+    part = nt(x_buf[...], q_buf[...].reshape(256, 512))
     for k in range(2):
         s_send[:, k, :] = part[:, 128 * k : 128 * k + 128]
     place = (me["x_lo"] * 2 + core) * 8 + tensor
@@ -312,7 +312,7 @@
 
     arrived(s_recv, s_rsem)
     for w in range(4):
-        scores_out[2 * w : 2 * w + 2, :] = jnp.sum(s_recv[8 * w : 8 * w + 8], axis=0)
+        scores_out[2 * w : 2 * w + 2, :] = jnp.sum(s_recv[8 * w : 8 * w + 8], axis=0) * (1.0 / 64)
     arrived(s_recv.at[pl.ds(0, 31)], s_ssem)
 
 

time: 31.6 us -> 31.6 us (level)
  no operation moved by 1% of the time
where the time goes in v7:
time: 31.6 us; the launch traced here: 31.5 us
  Pallas kernels  30.9 us (98%)
  between operations  0.64 us (2%)
    pallas_call x1, Pallas kernels, local(): pl.pallas_call(kernel, name='influence', out_shape=(jax.ShapeDtypeStruct(...  30.2 us

profile of v7, /device:TPU:1, one launch (start us, length us, event | category | flops | bytes accessed | tf_op | source)
XLA Modules:
  0.0 31.5 jit_solution(13079050661216960377)
XLA Ops:
  0.6 30.2 %influence.1 = (bf16[32,128]{1,0:T(8,128)(2,1)S(1)}, f32[8,128]{1,0:T(8,128)S(1)}) custom-call(bf16[8,128,1792]{2,1,0:T(8,128)(2,1)} %hidden.1, bf16[8,128,512]{2,1,0:T(8,128)(2,1)} %grads.1, bf16[64,1792]{1,0:T(8,128)(2,1)} %bitcast.2, bf16[64,512]{1,0:T(8,128)(2,1)} %bitcast.3, bf16[16,4096]{1,0:T(8,128)(2,1)} %queries.1), custom_call_target="tpu_custom_call" | custom-call | tf_op jit(solution)/shard_map/influence/pallas_call | solution.py:326
  30.9 0.6 %finish.1 = (bf16[1,4096]{1,0:T(2,128)(2,1)}, f32[1,1024]{1,0:T(1,128)}) custom-call(bf16[32,128]{1,0:T(8,128)(2,1)S(1)} %get-tuple-element.4.tg, f32[8,128]{1,0:T(8,128)S(1)} %get-tuple-element.5.part), custom_call_target="tpu_custom_call" | custom-call | tf_op jit(solution)/shard_map/finish/pallas_call | solution.py:356

commit v8 on v7

--- a/solution.py
+++ b/solution.py
@@ -187,6 +187,8 @@
 
     distant = jnp.logical_and(z >= 5, z < 8)
 
+    for d in (-4, 4, -3, 3, -2, 2, -1, 1):
+        when((z + d) // 8 == half, lambda d=d: near(d).start())
     for k, off in enumerate(TENSOR):
         example = device[difference(off, OPPOSITE)]["tensor"]
         if k == 7:
@@ -197,8 +199,6 @@
             device_id=device[off], device_id_type=MESH,
         ).start()
 
-    for d in (-4, 4, -3, 3, -2, 2, -1, 1):
-        when((z + d) // 8 == half, lambda d=d: near(d).start())
     when(distant, to_first_three)
     sibling = near(0, sib_ssem)
     own = pltpu.make_async_copy(mine, q_buf.at[slot], q_rsem)

time: 31.6 us -> 31.6 us (level)
  no operation moved by 1% of the time
where the time goes in v8:
time: 31.6 us; the launch traced here: 31.5 us
  Pallas kernels  30.9 us (98%)
  between operations  0.64 us (2%)
    pallas_call x1, Pallas kernels, local(): pl.pallas_call(kernel, name='influence', out_shape=(jax.ShapeDtypeStruct(...  30.2 us

profile of v8, /device:TPU:1, one launch (start us, length us, event | category | flops | bytes accessed | tf_op | source)
XLA Modules:
  0.0 31.5 jit_solution(16538385458916170324)
XLA Ops:
  0.6 30.2 %influence.1 = (bf16[32,128]{1,0:T(8,128)(2,1)S(1)}, f32[8,128]{1,0:T(8,128)S(1)}) custom-call(bf16[8,128,1792]{2,1,0:T(8,128)(2,1)} %hidden.1, bf16[8,128,512]{2,1,0:T(8,128)(2,1)} %grads.1, bf16[64,1792]{1,0:T(8,128)(2,1)} %bitcast.2, bf16[64,512]{1,0:T(8,128)(2,1)} %bitcast.3, bf16[16,4096]{1,0:T(8,128)(2,1)} %queries.1), custom_call_target="tpu_custom_call" | custom-call | tf_op jit(solution)/shard_map/influence/pallas_call | solution.py:326
  30.9 0.6 %finish.1 = (bf16[1,4096]{1,0:T(2,128)(2,1)}, f32[1,1024]{1,0:T(1,128)}) custom-call(bf16[32,128]{1,0:T(8,128)(2,1)S(1)} %get-tuple-element.4.tg, f32[8,128]{1,0:T(8,128)S(1)} %get-tuple-element.5.part), custom_call_target="tpu_custom_call" | custom-call | tf_op jit(solution)/shard_map/finish/pallas_call | solution.py:356
